TPU v7x, 32 devices: a whole 2x2x4 slice. The times are simulated.
32 devices in a mesh: grp: 4 (over x, core), orb: 8 (over z, y).
Axes of the slice: x: 2, y: 2, z: 4, core: 2. Of those that a mesh axis runs over, the one named last changes fastest.
Arguments:
- df_panels: bfloat16 [32, 1024, 512], P(('grp', 'orb')), may hold values from -1.0546875 to 1.0546875
- occ_energy: float32 [32], replicated, may hold values from -2 to -0.5
- virt_energy: float32 [512], replicated, may hold values from 0.2 to 4
- fock_off: float32 [512, 512], replicated, may hold values from -0.25 to 0.25
- i_plan: int32 [3, 4], replicated, may hold values from 0 to 7
- pair_owner: int32 [384, 1], P(('grp', 'orb')), may hold values from 0 to 3; in each aligned block of 12 rows (0 to 11, 12 to 23, ...) at most 4 rows name the same one
- pair_weight: float32 [384], P(('grp', 'orb')), may hold values from -4 to 4
Outputs:
- residual: float32 [32, 512, 512], P(('grp', 'orb'))
Inputs may be any that keep to these rules, and one draw needn't show every extreme that they name: `pair_owner`: each orbital's 12 rows name no group more than 4 times; some orbital names one group exactly 4 times.
All inputs are finite; a program needn't handle non-finite values.
Results may differ from a plain program's by a relative error of at most 0.0029.
Values may be sent and summed in bfloat16 or wider, within the bound.
A program may use at most 128 MiB of HBM per device.

v0:
```python
import jax
import jax.numpy as jnp
from jax import lax
from jax.sharding import PartitionSpec as P

NVIR = 512
STEPS = 3
CAP = 4


def from_root(value, axis, source):
    kept = jnp.where(lax.axis_index(axis) == source, value, 0).astype(value.dtype)
    return lax.psum(kept, axis)


def shards(df_panels, occ_energy, virt_energy, fock_off, i_plan, pair_owner, pair_weight):
    highest = lax.Precision.HIGHEST
    group_count = lax.axis_size("grp")
    orbit_count = lax.axis_size("orb")
    my_group = lax.axis_index("grp")
    my_orbital = my_group * orbit_count + lax.axis_index("orb")
    own_panel = df_panels[0]
    own_energy = lax.dynamic_index_in_dim(occ_energy, my_orbital, 0, keepdims=False)
    pair_sum = virt_energy[:, None] + virt_energy[None, :]
    groups_range = jnp.arange(group_count, dtype=jnp.int32)
    tiles = []
    for step_index in range(STEPS):
        pieces = []
        for group_index in range(group_count):
            source = group_index * orbit_count + i_plan[step_index, group_index]
            pieces.append(from_root(own_panel, ("grp", "orb"), source))
        gathered = jnp.stack(pieces, 0)
        i_ids = groups_range * orbit_count + i_plan[step_index]
        integral = jnp.einsum(
            "gxa,xb->gab", gathered, own_panel, preferred_element_type=jnp.float32
        )
        denominator = pair_sum[None] - occ_energy[i_ids][:, None, None] - own_energy
        tiles.append(integral / denominator)
    amplitude = (jnp.concatenate(tiles, 0) * pair_weight[:, None, None]).astype(jnp.bfloat16)
    tile_count = amplitude.shape[0]
    flat_tiles = amplitude.reshape(tile_count, NVIR * NVIR)
    owners = pair_owner[:, 0]
    one_hot = (owners[:, None] == groups_range[None, :]).astype(jnp.int32)
    slot_rank = jnp.sum((jnp.cumsum(one_hot, 0) - one_hot) * one_hot, 1)
    position = owners * CAP + slot_rank
    slot_range = jnp.arange(group_count * CAP, dtype=jnp.int32)
    selector = (position[None, :] == slot_range[:, None]).astype(jnp.bfloat16)
    send_tiles = jnp.dot(selector, flat_tiles, preferred_element_type=jnp.float32).astype(
        jnp.bfloat16
    )
    send_tiles = send_tiles.reshape(group_count, CAP, NVIR, NVIR)
    received = lax.all_to_all(send_tiles, "grp", split_axis=0, concat_axis=0, tiled=True)
    ones_row = jnp.ones((1, group_count * CAP), jnp.bfloat16)
    summed = jnp.dot(
        ones_row,
        received.reshape(group_count * CAP, NVIR * NVIR),
        preferred_element_type=jnp.float32,
    )
    summed = summed.reshape(NVIR, NVIR)
    fock_matrix = jnp.diag(virt_energy) + 0.5 * (fock_off + fock_off.T)
    left = jnp.dot(fock_matrix, summed, precision=highest)
    right = jnp.dot(summed, fock_matrix, precision=highest)
    return (left + right)[None]


def solution(mesh):
    placed = (
        P(("grp", "orb"), None, None),
        P(),
        P(),
        P(),
        P(),
        P(("grp", "orb"), None),
        P(("grp", "orb")),
    )
    return jax.shard_map(
        shards, mesh=mesh, in_specs=placed, out_specs=P(("grp", "orb"), None, None), check_vma=False
    )
```

profile of v0, /device:TPU:0, one launch (start us, length us, event | category | flops | bytes accessed | tf_op | source)
XLA Modules:
  0.0 428.9 jit_solution(3908849641237377064)
XLA Ops:
  6.5 1.8 fusion.72
  15.9 1.5 copy.19
  17.4 4.6 %fusion.43 = (bf16[1,1024,512]{1,2,0:T(8,128)(2,1)}, bf16[1,1024,512]{1,2,0:T(8,128)(2,1)}, bf16[1,1024,512]{1,2,0:T(8,128)(2,1)}, bf16[1,1024,512]{1,2,0:T(8,12...) fusion(bf16[1,1024,512]{1,2,0:T(8,128)(2,1)S(1)} %copy.19, ...), kind=kLoop, calls=%fused_computation.57 | loop fusion | flops 6291456 | bytes 13631500 | tf_op jit(solution)/shard_map/stack | solution.py:32
  22.1 0.6 copy-done
  22.7 0.6 dynamic_slice.4
  23.3 0.6 gather_fusion
  24.0 0.6 gather_fusion.1
  24.6 0.6 gather_fusion.2
  25.3 0.2 reduce_window_sum.11
  25.6 248.4 %all-reduce.3.cloned.1.call-done = (bf16[1,1024,512]{1,2,0:T(8,128)(2,1)}, bf16[1,1024,512]{1,2,0:T(8,128)(2,1)}, bf16[1,1024,512]{1,2,0:T(8,128)(2,1)}, bf16[1,...) async-done(((bf16[1,1024,512]{1,2,0:T(8,128)(2,1)}, ...) | async-done | bytes 12582928 | tf_op jit(solution)/shard_map/psum | solution.py:13
  274.1 4.9 %divide_bitcast_fusion.2 = f32[1,4,512,512]{3,2,1,0:T(8,128)S(1)} fusion(f32[]{:T(128)} %bitcast.15, f32[4]{0:T(128)S(1)} %gather_fusion, f32[512,512]{1,0:T(8,128)S(1)} %broadcast_add_fusion, bf16[1,1024,512]{1,2,0:T(8,128)(2,1)} %get-tuple-element.13, bf16[1,1024,512]{1,2,0:T(8,128)(2,1)} %get-tuple-element.14, ...), kind=kOutput, calls=%fused_computation.36 | convolution fusion | flops 2156920832 | bytes 10485780 | tf_op jit(solution)/shard_map/gxa,xb->gab/dot_general | solution.py:34
  279.0 2.7 copy.32
  281.8 3.4 divide_bitcast_fusion.1
  285.2 2.7 copy.33
  287.9 3.4 divide_bitcast_fusion
  291.3 2.9 copy.34
  294.3 5.9 %convolution_convert_fusion = bf16[16,262144]{1,0:T(8,128)(2,1)} fusion(f32[4,262144]{1,0:T(4,128)S(1)} %bitcast.150, f32[4,262144]{1,0:T(4,128)S(1)} %bitcast.149, f32[4,262144]{1,0:T(4,128)S(1)} %bitcast.148, f32[12]{0:T(128)S(1)} %copy-done.14, s32[12]{0:T(128)S(1)} %multiply_add_fusion), kind=kOutput, calls=%fused_computation.3 | convolution fusion | flops 117440704 | bytes 20971616 | tf_op jit(solution)/shard_map/dot_general | solution.py:48
  300.2 9.6 %copy.35 = bf16[2,8,512,512]{3,2,1,0:T(8,128)(2,1)} copy(bf16[2,8,512,512]{3,1,2,0:T(8,128)(2,1)} %bitcast.147) | data formatting | bytes 16777216
  309.8 5.8 %all-to-all-start = ((bf16[4,4,512,512]{3,2,1,0:T(8,128)(2,1)}), bf16[4,4,512,512]{3,2,1,0:T(8,128)(2,1)}, u32[]{:S(2)}, u32[]{:S(2)}) async-start(bf16[4,4,512,512]{3,2,1,0:T(8,128)(2,1)} %bitcast.146), calls=%async_computation | async-start | bytes 16777216 | tf_op jit(solution)/shard_map/all_to_all | solution.py:52
  315.6 0.3 copy.18
  316.0 92.8 %all-to-all-done = bf16[4,4,512,512]{3,2,1,0:T(8,128)(2,1)} async-done(((bf16[4,4,512,512]{3,2,1,0:T(8,128)(2,1)}), bf16[4,4,512,512]{3,2,1,0:T(8,128)(2,1)}, u32[]{:S(2)}, u32[]{:S(2)}) %all-to-all-start) | async-done | bytes 8388640 | tf_op jit(solution)/shard_map/all_to_all | solution.py:52
  408.8 8.4 %fusion.2 = f32[1,512,512]{2,0,1:T(1,128)S(1)} fusion(bf16[2,8,512,512]{3,2,1,0:T(8,128)(2,1)} %bitcast.56), kind=kOutput, calls=%fused_computation.6 | convolution fusion | flops 8388608 | bytes 9437184 | tf_op jit(solution)/shard_map/dot_general | solution.py:54
  417.1 1.9 fusion.41
  419.1 3.0 fusion.30
  (38 shorter events, 0.3 us)
Async XLA Ops:
  6.5 267.5 %all-reduce.3.cloned.1.call-start = ((), (), s32[]{:S(2)}) async-start(), calls=%async_computation.1 | async-start | bytes 25165824 | tf_op jit(solution)/shard_map/psum | solution.py:13
  22.1 0.7 copy-start
  22.1 1.2 copy-start.4
  22.1 3.2 copy-start.5
  22.1 3.4 copy-start.3
  22.1 251.9 %copy-start.2 = (bf16[1,1024,512]{2,1,0:T(8,128)(2,1)S(1)}, bf16[1,1024,512]{2,1,0:T(8,128)(2,1)}, u32[]{:S(2)}) copy-start(bf16[1,1024,512]{2,1,0:T(8,128)(2,1)} %param.7) | copy-start | bytes 3145732
  279.0 2.7 copy-start.10
  279.0 2.7 copy-start.11
  279.0 2.7 copy-start.12
  279.0 2.7 copy-start.13
  285.1 2.7 copy-start.6
  285.2 2.7 copy-start.7
  285.2 2.7 copy-start.8
  285.2 2.7 copy-start.9
  291.3 2.9 copy-start.14
  309.8 5.8 %copy-start.1 = (f32[512,512]{1,0:T(8,128)S(1)}, f32[512,512]{1,0:T(8,128)}, u32[]{:S(2)}) copy-start(f32[512,512]{1,0:T(8,128)} %param.10) | copy-start | bytes 3145732
  309.8 99.0 %all-to-all-start = ((bf16[4,4,512,512]{3,2,1,0:T(8,128)(2,1)}), bf16[4,4,512,512]{3,2,1,0:T(8,128)(2,1)}, u32[]{:S(2)}, u32[]{:S(2)}) async-start(bf16[4,4,512,512]{3,2,1,0:T(8,128)(2,1)} %bitcast.146), calls=%async_computation | async-start | bytes 16777216 | tf_op jit(solution)/shard_map/all_to_all | solution.py:52
Sparse Core Ops, SparseCore 0:
  22.3 251.7 all-reduce.2
where the time goes:
time: 429 us
  waiting for transfers between devices  341 us (79%)
  matrix products  30.8 us (7%)
  local copies, waits for them, and re-layouts  24.7 us (6%)
  between operations  21.3 us (5%)
  starting transfers between devices  5.81 us (1%)
  other arithmetic  5.01 us (1%)
    psum x1, waiting for transfers between devices, from_root(): return lax.psum(kept, axis)  248 us
    all_to_all x1, waiting for transfers between devices, shards(): lax.all_to_all(send_tiles, 'grp', split_axis=0, concat_axis=0, tiled=True)  92.8 us
    unnamed x36, local copies, waits for them, and re-layouts  20.4 us
    dot_general x3, matrix products, shards(): jnp.einsum('gxa,xb->gab', gathered, own_panel, preferred_element_type=jnp...  11.7 us
  transfers between devices with their start and end apart: 2, of which 2 were waited for; matrix products, arithmetic and copies ran while one was open for 1% of the time, Pallas kernels for 0%

commit v1 on v0

v1 whole, which is shorter than its diff:
```python
import functools

import jax
import jax.numpy as jnp
from jax import lax
from jax.experimental import pallas as pl
from jax.experimental.pallas import tpu as pltpu
from jax.sharding import PartitionSpec as P

MESH = pl.DeviceIdType.MESH
ROWS = 8


def ring_orb(pos, n):
    half = n // 2
    return jnp.where(pos < half, 2 * pos, 2 * (n - 1 - pos) + 1)


def gather_kernel(
    ng, no, nt, ids, panel_t, panel, meta, gt, cols, metas,
    pieces, sel, sc_send, sc_recv, col_send, col_recv, meta_send, meta_recv,
    ring_send, ring_recv, loc,
):
    nall = ng * no
    g = lax.axis_index("grp")
    o = lax.axis_index("orb")
    me = g * no + o
    nvir, naux = panel_t.shape
    qa = nvir // ng
    ra = qa // ROWS
    nc = no // ROWS
    wa = naux // nc
    half_t = nt // 2

    def piece_of(orb):
        return orb // nc, orb % nc

    def block_in_panel(q, orb):
        r, c = piece_of(orb)
        return panel_t.at[
            pl.ds(pl.multiple_of(q * qa + r * ra, 16), ra), pl.ds(pl.multiple_of(c * wa, 128), wa)
        ]

    def scatter(k):
        to = lax.rem(me + k, nall)
        q, orb = to // no, lax.rem(to, no)
        return pltpu.make_async_remote_copy(
            src_ref=block_in_panel(q, orb),
            dst_ref=pieces.at[me],
            send_sem=sc_send.at[k],
            recv_sem=sc_recv.at[k],
            device_id=(q, orb),
            device_id_type=MESH,
        )

    own_piece = pltpu.make_async_copy(block_in_panel(g, o), pieces.at[me], loc.at[0])
    own_piece.start()

    def start_scatter(k, carry):
        scatter(k).start()
        return carry

    lax.fori_loop(1, nall, start_scatter, 0)

    gx, gc = g // 2, lax.rem(g, 2)
    core_peer = gx * 2 + 1 - gc
    x_peer = (1 - gx) * 2 + gc
    diag_peer = (1 - gx) * 2 + 1 - gc

    def column(index, src, slot, to):
        return pltpu.make_async_remote_copy(
            src_ref=src,
            dst_ref=cols.at[slot],
            send_sem=col_send.at[index],
            recv_sem=col_recv.at[index],
            device_id=(to, o),
            device_id_type=MESH,
        )

    across = column(0, panel, g, x_peer)
    beside = column(1, panel, g, core_peer)
    across.start()
    beside.start()
    own_col = pltpu.make_async_copy(panel, cols.at[g], loc.at[1])
    own_col.start()
    own_meta = pltpu.make_async_copy(meta, metas.at[g], loc.at[2])
    own_meta.start()
    meta_copies = []
    for index, to in enumerate((core_peer, x_peer, diag_peer)):
        copy = pltpu.make_async_remote_copy(
            src_ref=meta,
            dst_ref=metas.at[g],
            send_sem=meta_send.at[index],
            recv_sem=meta_recv.at[index],
            device_id=(to, o),
            device_id_type=MESH,
        )
        copy.start()
        meta_copies.append(copy)

    own_piece.wait()

    def wait_scatter(k, carry):
        scatter(k).wait_recv()
        return carry

    lax.fori_loop(1, nall, wait_scatter, 0)
    for t in range(nt):
        sel[t] = pieces[ids[t]]

    def block_in_gt(hf, orb):
        r, c = piece_of(orb)
        return gt.at[
            pl.ds(hf * half_t, half_t),
            pl.ds(pl.multiple_of(r * ra, 16), ra),
            pl.ds(pl.multiple_of(c * wa, 128), wa),
        ]

    r_me, c_me = piece_of(o)
    own_sel = pltpu.make_async_copy(
        sel,
        gt.at[
            :, pl.ds(pl.multiple_of(r_me * ra, 16), ra), pl.ds(pl.multiple_of(c_me * wa, 128), wa)
        ],
        loc.at[3],
    )
    own_sel.start()

    pos = jnp.where(lax.rem(o, 2) == 0, o // 2, no - 1 - o // 2)
    steps = no // 2
    next_orb = (
        ring_orb(lax.rem(pos + 1, no), no),
        ring_orb(lax.rem(pos + no - 1, no), no),
    )

    def ring(way, step, hf):
        origin = lax.rem(pos + (no - step if way == 0 else step), no)
        orb = ring_orb(origin, no)
        src = block_in_gt(hf, orb)
        if step == 0:
            src = sel.at[pl.ds(hf * half_t, half_t)]
        return pltpu.make_async_remote_copy(
            src_ref=src,
            dst_ref=block_in_gt(hf, orb),
            send_sem=ring_send.at[way, step, hf],
            recv_sem=ring_recv.at[way, step, hf],
            device_id=(g, next_orb[way]),
            device_id_type=MESH,
        )

    def used(way, step, hf):
        return step < steps - 1 or hf == way

    for step in range(steps):
        for hf in range(2):
            for way in range(2):
                if used(way, step, hf):
                    if step > 0:
                        ring(way, step - 1, hf).wait_recv()
                    ring(way, step, hf).start()
        if step == 0:
            across.wait_recv()
            onward = column(2, cols.at[x_peer], x_peer, core_peer)
            onward.start()

    for way in range(2):
        for step in range(steps):
            for hf in range(2):
                if used(way, step, hf):
                    if step == steps - 1 or not used(way, step + 1, hf):
                        ring(way, step, hf).wait_recv()
    beside.wait_recv()
    onward.wait_recv()
    for copy in meta_copies:
        copy.wait_recv()

    def wait_sent(k, carry):
        scatter(k).wait_send()
        return carry

    lax.fori_loop(1, nall, wait_sent, 0)
    across.wait_send()
    beside.wait_send()
    onward.wait_send()
    for copy in meta_copies:
        copy.wait_send()
    for way in range(2):
        for step in range(steps):
            for hf in range(2):
                if used(way, step, hf):
                    ring(way, step, hf).wait_send()
    own_col.wait()
    own_meta.wait()
    own_sel.wait()


def tiles_kernel(nt, metas, occ_i, gt, col, va, vb, out, acc):
    j = pl.program_id(0)
    ng = out.shape[0]
    qa = gt.shape[1]
    group = 4

    @pl.when(j == 0)
    def _():
        acc[...] = jnp.zeros_like(acc)

    base = va[...] + vb[...]
    own = metas[j, 0, 2 * nt]
    right = col[0]
    for first in range(0, nt, group):
        left = gt[first : first + group].reshape(group * qa, gt.shape[2])
        integral = jnp.dot(left, right, preferred_element_type=jnp.float32)
        for k in range(group):
            t = first + k
            weight = metas[j, 0, t]
            owner = metas[j, 0, nt + t].astype(jnp.int32)
            denominator = base - occ_i[t] - own
            amplitude = integral[k * qa : (k + 1) * qa] / denominator * weight
            acc[owner] = acc[owner] + amplitude.astype(jnp.bfloat16).astype(jnp.float32)

    @pl.when(j == ng - 1)
    def _():
        out[...] = acc[...].astype(out.dtype)


def fock_kernel(summed, high, low, out):
    s = summed[...]
    h = high[...]
    l = low[...]
    dot = functools.partial(jnp.dot, preferred_element_type=jnp.float32)
    out[...] = (dot(h, s) + dot(s, h)) + (dot(l, s) + dot(s, l))


def shards(df_panels, occ_energy, virt_energy, fock_off, i_plan, pair_owner, pair_weight):
    ng = lax.axis_size("grp")
    no = lax.axis_size("orb")
    g = lax.axis_index("grp")
    me = g * no + lax.axis_index("orb")
    panel = df_panels[0]
    naux, nvir = panel.shape
    nt = pair_owner.shape[0]
    qa = nvir // ng
    f32 = jnp.float32
    vmem = pl.BlockSpec(memory_space=pltpu.VMEM)
    smem = pl.BlockSpec(memory_space=pltpu.SMEM)
    hbm = pl.BlockSpec(memory_space=pl.ANY)
    dma = pltpu.SemaphoreType.DMA

    ids = (jnp.arange(ng, dtype=jnp.int32)[None, :] * no + i_plan).reshape(nt)
    own_energy = lax.dynamic_slice_in_dim(occ_energy, me, 1)
    row = jnp.concatenate([pair_weight, pair_owner[:, 0].astype(f32), own_energy])
    meta = jnp.zeros((8, 128), f32).at[0, : 2 * nt + 1].set(row)
    nc = no // ROWS
    gt, cols, metas = pl.pallas_call(
        functools.partial(gather_kernel, ng, no, nt),
        out_shape=[
            jax.ShapeDtypeStruct((nt, qa, naux), jnp.bfloat16),
            jax.ShapeDtypeStruct((ng, naux, nvir), jnp.bfloat16),
            jax.ShapeDtypeStruct((ng, 8, 128), f32),
        ],
        in_specs=[smem, hbm, hbm, hbm],
        out_specs=[hbm, hbm, hbm],
        scratch_shapes=[
            pltpu.VMEM((ng * no, qa // ROWS, naux // nc), jnp.bfloat16),
            pltpu.VMEM((nt, qa // ROWS, naux // nc), jnp.bfloat16),
            dma((ng * no,)),
            dma((ng * no,)),
            dma((3,)),
            dma((3,)),
            dma((3,)),
            dma((3,)),
            dma((2, no // 2, 2)),
            dma((2, no // 2, 2)),
            dma((4,)),
        ],
        compiler_params=pltpu.CompilerParams(has_side_effects=True),
        name="gather_panels",
    )(ids, panel.T, panel, meta)

    va = lax.dynamic_slice_in_dim(virt_energy, g * qa, qa)[:, None]
    parts = pl.pallas_call(
        functools.partial(tiles_kernel, nt),
        grid=(ng,),
        out_shape=jax.ShapeDtypeStruct((ng, qa, nvir), jnp.bfloat16),
        in_specs=[
            smem,
            smem,
            vmem,
            pl.BlockSpec((1, naux, nvir), lambda j: (j, 0, 0)),
            vmem,
            vmem,
        ],
        out_specs=vmem,
        scratch_shapes=[pltpu.VMEM((ng, qa, nvir), f32)],
        compiler_params=pltpu.CompilerParams(vmem_limit_bytes=48 * 2**20),
        name="pair_tiles",
    )(metas[:, :1, :], occ_energy[ids], gt, cols, va, virt_energy[None, :])

    summed = lax.all_to_all(parts, "grp", split_axis=0, concat_axis=0, tiled=True)
    summed = summed.reshape(nvir, nvir)
    fock = jnp.diag(virt_energy) + 0.5 * (fock_off + fock_off.T)
    high = fock.astype(jnp.bfloat16)
    low = (fock - high.astype(f32)).astype(jnp.bfloat16)
    residual = pl.pallas_call(
        fock_kernel,
        out_shape=jax.ShapeDtypeStruct((nvir, nvir), f32),
        in_specs=[vmem] * 3,
        out_specs=vmem,
        compiler_params=pltpu.CompilerParams(vmem_limit_bytes=48 * 2**20),
        name="fock_products",
    )(summed, high, low)
    return residual[None]


def solution(mesh):
    placed = (
        P(("grp", "orb"), None, None),
        P(),
        P(),
        P(),
        P(),
        P(("grp", "orb"), None),
        P(("grp", "orb")),
    )
    return jax.shard_map(
        shards, mesh=mesh, in_specs=placed, out_specs=P(("grp", "orb"), None, None), check_vma=False
    )
```

time: 429 us -> 107 us (0.25)
  waiting for transfers between devices: 341 us -> 5.94 us
  Pallas kernels: 0 us -> 83.6 us
  matrix products: 30.8 us -> 0 us
  between operations: 21.3 us -> 0.07 us
  local copies, waits for them, and re-layouts: 24.7 us -> 9.59 us
    psum x1 -> x0, waiting for transfers between devices: 248 us -> none  [from_root(): return lax.psum(kept, axis)]
    all_to_all x1, waiting for transfers between devices: 92.8 us -> 5.94 us  [shards(): lax.all_to_all(parts, 'grp', split_axis=0, concat_axis=0, tiled=True)]
    pallas_call x0 -> x3, Pallas kernels: none -> 83.6 us  [the longest x1 70.5 us: shards(): pl.pallas_call(functools.partial(gather_kernel, ng, no, nt), out_shape=[j...]
    dot_general x7 -> x0, matrix products: 30.8 us -> none  [the longest x3 11.7 us: shards(): jnp.einsum('gxa,xb->gab', gathered, own_panel, preferred_element_type=jnp...]
    unnamed x36 -> x9, local copies, waits for them, and re-layouts: 20.4 us -> 3.21 us
  transfers between devices with their start and end apart: 2 -> 1, of which waited for: 2 -> 1; matrix products, arithmetic and copies ran while one was open for 1% -> 3% of each run, Pallas kernels for 0% -> 0%
where the time goes in v1:
time: 107 us
  Pallas kernels  83.6 us (78%)
  local copies, waits for them, and re-layouts  9.59 us (9%)
  waiting for transfers between devices  5.94 us (6%)
  other arithmetic  4.21 us (4%)
  starting transfers between devices  3.47 us (3%)
    pallas_call x1, Pallas kernels, shards(): pl.pallas_call(functools.partial(gather_kernel, ng, no, nt), out_shape=[j...  70.5 us
    pallas_call x1, Pallas kernels, shards(): pl.pallas_call(functools.partial(tiles_kernel, nt), grid=(ng,), out_shape...  10.9 us
    all_to_all x1, waiting for transfers between devices, shards(): lax.all_to_all(parts, 'grp', split_axis=0, concat_axis=0, tiled=True)  5.94 us
    all_to_all x1, starting transfers between devices, shards(): lax.all_to_all(parts, 'grp', split_axis=0, concat_axis=0, tiled=True)  3.47 us
    unnamed x9, local copies, waits for them, and re-layouts  3.21 us
    transpose x1, local copies, waits for them, and re-layouts, shards(): gt, cols, metas = pl.pallas_call(functools.partial(gather_kernel, ng, no,...  2.26 us
    pallas_call x1, Pallas kernels, shards(): pl.pallas_call(fock_kernel, out_shape=jax.ShapeDtypeStruct((nvir, nvir),...  2.22 us
  transfers between devices with their start and end apart: 1, of which 1 were waited for; matrix products, arithmetic and copies ran while one was open for 3% of the time, Pallas kernels for 0%

profile of v1, /device:TPU:0, one launch (start us, length us, event | category | flops | bytes accessed | tf_op | source)
XLA Modules:
  0.0 106.9 jit_solution(13357222109844816872)
XLA Ops:
  0.0 0.0 copy-start.2
  0.0 0.7 broadcast_add_fusion
  0.7 0.7 reshape.73.ids
  1.4 0.1 reshape.75
  1.5 0.7 convert_bitcast_fusion
  2.1 2.3 %copy.11.panel_t = bf16[512,1024]{1,0:T(8,128)(2,1)} copy(bf16[512,1024]{0,1:T(8,128)(2,1)} %bitcast.28) | data formatting | bytes 2097152 | tf_op jit(solution)/shard_map/transpose | solution.py:278
  4.4 1.2 %dynamic_slice.6 = f32[1]{0:T(128)} dynamic-slice(f32[32]{0:T(128)} %param.10, s32[]{:T(128)S(6)} %select_n.21), dynamic_slice_sizes={1} | dynamic-slice | bytes 12 | tf_op jit(solution)/shard_map/dynamic_slice | solution.py:250
  5.6 1.3 %maximum_bitcast_fusion = f32[1,25]{1,0:T(1,128)S(1)} fusion(f32[1]{0:T(128)} %dynamic_slice.6, f32[12]{0:T(128)S(1)} %convert_bitcast_fusion, f32[12]{0:T(128)} %param.15), kind=kLoop, calls=%fused_computation.10 | loop fusion | flops 50 | bytes 200 | tf_op jit(solution)/shard_map/reshape.31
  6.9 0.6 scatter.4.meta
  7.5 70.5 %gather_panels.1 = (bf16[12,128,1024]{2,1,0:T(8,128)(2,1)}, bf16[4,1024,512]{2,1,0:T(8,128)(2,1)}, f32[4,8,128]{2,1,0:T(8,128)}) custom-call(s32[12]{0:T(128)} %reshape.73.ids, bf16[512,1024]{1,0:T(8,128)(2,1)} %copy.11.panel_t, bf16[1024,512]{1,0:T(8,128)(2,1)} %bitcast.29, f32[8,128]{1,0:T(8,128)} %scatter.4.meta), custom_call_target="tpu_custom_call" | custom-call | tf_op jit(solution)/shard_map/gather_panels/pallas_call | solution.py:254
  78.0 0.7 slice.19.metas
  78.7 0.0 copy-done.1
  78.7 0.1 dynamic-slice_bitcast_fusion
  78.8 0.1 copy.12.va
  79.0 0.0 copy-done.2
  79.0 0.7 gather_fusion
  79.6 1.9 %copy-done = bf16[12,128,1024]{2,1,0:T(8,128)(2,1)S(1)} copy-done((bf16[12,128,1024]{2,1,0:T(8,128)(2,1)S(1)}, bf16[12,128,1024]{2,1,0:T(8,128)(2,1)}, u32[]{:S(2)}) %copy-start) | copy-done | bytes 3145752
  81.5 10.9 %pair_tiles.1 = bf16[4,128,512]{2,1,0:T(8,128)(2,1)} custom-call(f32[4,1,128]{2,1,0:T(1,128)S(1)} %slice.19.metas, f32[12]{0:T(128)S(1)} %gather_fusion, bf16[12,128,1024]{2,1,0:T(8,128)(2,1)S(1)} %copy-done, bf16[4,1024,512]{2,1,0:T(8,128)(2,1)} %get-tuple-element.22.col, f32[128,1]{1,0:T(8,128)S(1)} %copy.12.va, f32[1,512]{1,0:T(1,128)S(1)} %bitcast.27), custom_call_target="tpu_custom_call" | custom-call | tf_op jit(solution)/shard_map/pair_tiles/pallas_call | solution.py:281
  92.4 3.5 %all-to-all-start = ((bf16[4,128,512]{2,1,0:T(8,128)(2,1)}), bf16[4,128,512]{2,1,0:T(8,128)(2,1)S(1)}, u32[]{:S(2)}, u32[]{:S(2)}) async-start(bf16[4,128,512]{2,1,0:T(8,128)(2,1)} %pair_tiles.1), calls=%async_computation | async-start | bytes 1048576 | tf_op jit(solution)/shard_map/all_to_all | solution.py:299
  95.9 0.0 copy-done.3
  95.9 1.3 %copy.13 = f32[512,512]{0,1:T(8,128)} copy(f32[512,512]{1,0:T(8,128)S(1)} %copy-done.3) | data formatting | bytes 2097152 | tf_op args[3]
  97.2 1.5 %subtract_convert_fusion = (bf16[512,512]{1,0:T(8,128)(2,1)S(1)}, bf16[512,512]{1,0:T(8,128)(2,1)S(1)}) fusion(f32[512,512]{1,0:T(8,128)S(1)} %copy-done.3, f32[512,512]{0,1:T(8,128)} %copy.13, f32[512]{0:T(512)S(1)} %copy-done.1), kind=kLoop, calls=%fused_computation.4 | loop fusion | flops 2359296 | bytes 3147776 | tf_op jit(solution)/shard_map/convert_element_type | solution.py:303
  98.7 5.9 %all-to-all-done = bf16[4,128,512]{2,1,0:T(8,128)(2,1)S(1)} async-done(((bf16[4,128,512]{2,1,0:T(8,128)(2,1)}), bf16[4,128,512]{2,1,0:T(8,128)(2,1)S(1)}, u32[]{:S(2)}, u32[]{:S(2)}) %all-to-all-start) | async-done | bytes 524320 | tf_op jit(solution)/shard_map/all_to_all | solution.py:299
  104.7 2.2 %fock_products.1 = f32[512,512]{1,0:T(8,128)} custom-call(bf16[512,512]{1,0:T(8,128)(2,1)S(1)} %bitcast.26, bf16[512,512]{1,0:T(8,128)(2,1)S(1)} %get-tuple-element.24.high, bf16[512,512]{1,0:T(8,128)(2,1)S(1)} %get-tuple-element.23.low), custom_call_target="tpu_custom_call" | custom-call | tf_op jit(solution)/shard_map/fock_products/pallas_call | solution.py:304
  (6 shorter events, 0.0 us)
Async XLA Ops:
  0.0 79.0 %copy-start.2 = (f32[32]{0:T(128)S(1)}, f32[32]{0:T(128)}, u32[]{:S(2)}) copy-start(f32[32]{0:T(128)} %param.10) | copy-start | bytes 388
  0.0 78.7 %copy-start.1 = (f32[512]{0:T(512)S(1)}, f32[512]{0:T(512)}, u32[]{:S(2)}) copy-start(f32[512]{0:T(512)} %param.11) | copy-start | bytes 6148
  79.6 1.9 %copy-start = (bf16[12,128,1024]{2,1,0:T(8,128)(2,1)S(1)}, bf16[12,128,1024]{2,1,0:T(8,128)(2,1)}, u32[]{:S(2)}) copy-start(bf16[12,128,1024]{2,1,0:T(8,128)(2,1)} %get-tuple-element.21.gt) | copy-start | bytes 9437188
  81.5 14.4 %copy-start.3 = (f32[512,512]{1,0:T(8,128)S(1)}, f32[512,512]{1,0:T(8,128)}, u32[]{:S(2)}) copy-start(f32[512,512]{1,0:T(8,128)} %param.12) | copy-start | bytes 3145732
  92.4 12.3 %all-to-all-start = ((bf16[4,128,512]{2,1,0:T(8,128)(2,1)}), bf16[4,128,512]{2,1,0:T(8,128)(2,1)S(1)}, u32[]{:S(2)}, u32[]{:S(2)}) async-start(bf16[4,128,512]{2,1,0:T(8,128)(2,1)} %pair_tiles.1), calls=%async_computation | async-start | bytes 1048576 | tf_op jit(solution)/shard_map/all_to_all | solution.py:299

commit v2 on v1

--- a/solution.py
+++ b/solution.py
@@ -17,14 +17,12 @@
 
 
 def gather_kernel(
-    ng, no, nt, ids, panel_t, panel, meta, gt, cols, metas,
-    pieces, sel, sc_send, sc_recv, col_send, col_recv, meta_send, meta_recv,
+    ng, no, nt, plan, weight, owner, panel_t, panel, gt, cols, metas,
+    meta, pieces_here, pieces_over, sel, sc_send, sc_recv, col_send, col_recv, meta_send, meta_recv,
     ring_send, ring_recv, loc,
 ):
-    nall = ng * no
     g = lax.axis_index("grp")
     o = lax.axis_index("orb")
-    me = g * no + o
     nvir, naux = panel_t.shape
     qa = nvir // ng
     ra = qa // ROWS
@@ -41,28 +39,39 @@
             pl.ds(pl.multiple_of(q * qa + r * ra, 16), ra), pl.ds(pl.multiple_of(c * wa, 128), wa)
         ]
 
-    def scatter(k):
-        to = lax.rem(me + k, nall)
+    pieces = (pieces_here, pieces_over)
+    gx, gc = g // 2, lax.rem(g, 2)
+    side = 2 * no
+    place = gc * no + o
+
+    def scatter(hf, k):
+        to = lax.rem(gx + hf, 2) * side + lax.rem(place + k, side)
         q, orb = to // no, lax.rem(to, no)
         return pltpu.make_async_remote_copy(
             src_ref=block_in_panel(q, orb),
-            dst_ref=pieces.at[me],
-            send_sem=sc_send.at[k],
-            recv_sem=sc_recv.at[k],
+            dst_ref=pieces[hf].at[place],
+            send_sem=sc_send.at[hf, k],
+            recv_sem=sc_recv.at[hf, k],
             device_id=(q, orb),
             device_id_type=MESH,
         )
 
-    own_piece = pltpu.make_async_copy(block_in_panel(g, o), pieces.at[me], loc.at[0])
+    own_piece = pltpu.make_async_copy(block_in_panel(g, o), pieces_here.at[place], loc.at[0])
     own_piece.start()
 
-    def start_scatter(k, carry):
-        scatter(k).start()
-        return carry
-
-    lax.fori_loop(1, nall, start_scatter, 0)
-
-    gx, gc = g // 2, lax.rem(g, 2)
+    def each_scatter(hf, act):
+        def body(k, carry):
+            act(scatter(hf, k))
+            return carry
+
+        lax.fori_loop(1 - hf, side, body, 0)
+
+    each_scatter(0, lambda copy: copy.start())
+    each_scatter(1, lambda copy: copy.start())
+    meta[...] = jnp.zeros_like(meta)
+    meta[0:1, 0:nt] = weight[...]
+    meta[1:2, 0:nt] = owner[...].astype(jnp.float32)
+
     core_peer = gx * 2 + 1 - gc
     x_peer = (1 - gx) * 2 + gc
     diag_peer = (1 - gx) * 2 + 1 - gc
@@ -100,13 +109,12 @@
 
     own_piece.wait()
 
-    def wait_scatter(k, carry):
-        scatter(k).wait_recv()
-        return carry
-
-    lax.fori_loop(1, nall, wait_scatter, 0)
-    for t in range(nt):
-        sel[t] = pieces[ids[t]]
+    def select(hf):
+        side_x = lax.rem(gx + hf, 2)
+        for c in range(2):
+            for s in range(nt // ng):
+                h = side_x * 2 + c
+                sel[hf * half_t + c * (nt // ng) + s] = pieces[hf][c * no + plan[s, h]]
 
     def block_in_gt(hf, orb):
         r, c = piece_of(orb)
@@ -116,15 +124,12 @@
             pl.ds(pl.multiple_of(c * wa, 128), wa),
         ]
 
-    r_me, c_me = piece_of(o)
-    own_sel = pltpu.make_async_copy(
-        sel,
-        gt.at[
-            :, pl.ds(pl.multiple_of(r_me * ra, 16), ra), pl.ds(pl.multiple_of(c_me * wa, 128), wa)
-        ],
-        loc.at[3],
-    )
-    own_sel.start()
+    own_sel = [
+        pltpu.make_async_copy(
+            sel.at[pl.ds(hf * half_t, half_t)], block_in_gt(hf, o), loc.at[3 + hf]
+        )
+        for hf in range(2)
+    ]
 
     pos = jnp.where(lax.rem(o, 2) == 0, o // 2, no - 1 - o // 2)
     steps = no // 2
@@ -153,6 +158,10 @@
 
     for step in range(steps):
         for hf in range(2):
+            if step == 0:
+                each_scatter(hf, lambda copy: copy.wait_recv())
+                select(hf)
+                own_sel[hf].start()
             for way in range(2):
                 if used(way, step, hf):
                     if step > 0:
@@ -174,11 +183,8 @@
     for copy in meta_copies:
         copy.wait_recv()
 
-    def wait_sent(k, carry):
-        scatter(k).wait_send()
-        return carry
-
-    lax.fori_loop(1, nall, wait_sent, 0)
+    each_scatter(0, lambda copy: copy.wait_send())
+    each_scatter(1, lambda copy: copy.wait_send())
     across.wait_send()
     beside.wait_send()
     onward.wait_send()
@@ -191,36 +197,55 @@
                     ring(way, step, hf).wait_send()
     own_col.wait()
     own_meta.wait()
-    own_sel.wait()
-
-
-def tiles_kernel(nt, metas, occ_i, gt, col, va, vb, out, acc):
-    j = pl.program_id(0)
+    for copy in own_sel:
+        copy.wait()
+
+
+def tiles_kernel(nt, group, no, metas, plan, occ, gt, cols, virt, out, acc, base):
+    part = pl.program_id(0)
+    j = pl.program_id(1)
     ng = out.shape[0]
     qa = gt.shape[1]
-    group = 4
-
-    @pl.when(j == 0)
+    steps = nt // ng
+    g = lax.axis_index("grp")
+    o = lax.axis_index("orb")
+
+    @pl.when((j == 0) & (part == 0))
     def _():
         acc[...] = jnp.zeros_like(acc)
-
-    base = va[...] + vb[...]
-    own = metas[j, 0, 2 * nt]
-    right = col[0]
-    for first in range(0, nt, group):
-        left = gt[first : first + group].reshape(group * qa, gt.shape[2])
-        integral = jnp.dot(left, right, preferred_element_type=jnp.float32)
-        for k in range(group):
-            t = first + k
-            weight = metas[j, 0, t]
-            owner = metas[j, 0, nt + t].astype(jnp.int32)
-            denominator = base - occ_i[t] - own
-            amplitude = integral[k * qa : (k + 1) * qa] / denominator * weight
-            acc[owner] = acc[owner] + amplitude.astype(jnp.bfloat16).astype(jnp.float32)
-
-    @pl.when(j == ng - 1)
+        rows = jnp.broadcast_to(virt[:, pl.ds(pl.multiple_of(g * qa, 128), qa)], (qa, qa)).T
+        for k in range(out.shape[2] // qa):
+            at = slice(k * qa, (k + 1) * qa)
+            base[:, at] = rows + virt[:, at]
+
+    own = occ[j * no + o]
+    left = gt[...].reshape(group * qa, gt.shape[2])
+    integral = jnp.dot(left, cols[0], preferred_element_type=jnp.float32)
+    for k in range(group):
+        slot = part * group + k
+        hf, rest = slot // (nt // 2), lax.rem(slot, nt // 2)
+        c, s = rest // steps, lax.rem(rest, steps)
+        h = lax.rem(g // 2 + hf, 2) * 2 + c
+        t = s * ng + h
+        weight = metas[j, 0, t]
+        owner = metas[j, 1, t].astype(jnp.int32)
+        denominator = base[...] - occ[h * no + plan[s, h]] - own
+        amplitude = integral[k * qa : (k + 1) * qa] / denominator * weight
+        acc[owner] = acc[owner] + amplitude.astype(jnp.bfloat16).astype(jnp.float32)
+
+    @pl.when((j == ng - 1) & (part == pl.num_programs(0) - 1))
     def _():
         out[...] = acc[...].astype(out.dtype)
+
+
+def split_kernel(virt, off, high, low):
+    n = off.shape[0]
+    rows = lax.broadcasted_iota(jnp.int32, (n, n), 0)
+    columns = lax.broadcasted_iota(jnp.int32, (n, n), 1)
+    fock = jnp.where(rows == columns, virt[...], 0.0) + 0.5 * (off[...] + off[...].T)
+    top = fock.astype(jnp.bfloat16)
+    high[...] = top
+    low[...] = (fock - top.astype(jnp.float32)).astype(jnp.bfloat16)
 
 
 def fock_kernel(summed, high, low, out):
@@ -234,8 +259,6 @@
 def shards(df_panels, occ_energy, virt_energy, fock_off, i_plan, pair_owner, pair_weight):
     ng = lax.axis_size("grp")
     no = lax.axis_size("orb")
-    g = lax.axis_index("grp")
-    me = g * no + lax.axis_index("orb")
     panel = df_panels[0]
     naux, nvir = panel.shape
     nt = pair_owner.shape[0]
@@ -246,10 +269,6 @@
     hbm = pl.BlockSpec(memory_space=pl.ANY)
     dma = pltpu.SemaphoreType.DMA
 
-    ids = (jnp.arange(ng, dtype=jnp.int32)[None, :] * no + i_plan).reshape(nt)
-    own_energy = lax.dynamic_slice_in_dim(occ_energy, me, 1)
-    row = jnp.concatenate([pair_weight, pair_owner[:, 0].astype(f32), own_energy])
-    meta = jnp.zeros((8, 128), f32).at[0, : 2 * nt + 1].set(row)
     nc = no // ROWS
     gt, cols, metas = pl.pallas_call(
         functools.partial(gather_kernel, ng, no, nt),
@@ -258,49 +277,57 @@
             jax.ShapeDtypeStruct((ng, naux, nvir), jnp.bfloat16),
             jax.ShapeDtypeStruct((ng, 8, 128), f32),
         ],
-        in_specs=[smem, hbm, hbm, hbm],
+        in_specs=[smem, vmem, vmem, hbm, hbm],
         out_specs=[hbm, hbm, hbm],
         scratch_shapes=[
-            pltpu.VMEM((ng * no, qa // ROWS, naux // nc), jnp.bfloat16),
+            pltpu.VMEM((8, 128), f32),
+            pltpu.VMEM((2 * no, qa // ROWS, naux // nc), jnp.bfloat16),
+            pltpu.VMEM((2 * no, qa // ROWS, naux // nc), jnp.bfloat16),
             pltpu.VMEM((nt, qa // ROWS, naux // nc), jnp.bfloat16),
-            dma((ng * no,)),
-            dma((ng * no,)),
+            dma((2, 2 * no)),
+            dma((2, 2 * no)),
             dma((3,)),
             dma((3,)),
             dma((3,)),
             dma((3,)),
             dma((2, no // 2, 2)),
             dma((2, no // 2, 2)),
-            dma((4,)),
+            dma((5,)),
         ],
         compiler_params=pltpu.CompilerParams(has_side_effects=True),
         name="gather_panels",
-    )(ids, panel.T, panel, meta)
-
-    va = lax.dynamic_slice_in_dim(virt_energy, g * qa, qa)[:, None]
+    )(i_plan, pair_weight.reshape(1, nt), pair_owner.reshape(1, nt), panel.T, panel)
+
+    virt_row = virt_energy[None, :]
+    group = 4
     parts = pl.pallas_call(
-        functools.partial(tiles_kernel, nt),
-        grid=(ng,),
+        functools.partial(tiles_kernel, nt, group, no),
+        grid=(nt // group, ng),
         out_shape=jax.ShapeDtypeStruct((ng, qa, nvir), jnp.bfloat16),
         in_specs=[
             smem,
             smem,
-            vmem,
-            pl.BlockSpec((1, naux, nvir), lambda j: (j, 0, 0)),
-            vmem,
+            smem,
+            pl.BlockSpec((group, qa, naux), lambda p, j: (p, 0, 0)),
+            pl.BlockSpec((1, naux, nvir), lambda p, j: (j, 0, 0)),
             vmem,
         ],
         out_specs=vmem,
-        scratch_shapes=[pltpu.VMEM((ng, qa, nvir), f32)],
-        compiler_params=pltpu.CompilerParams(vmem_limit_bytes=48 * 2**20),
+        scratch_shapes=[pltpu.VMEM((ng, qa, nvir), f32), pltpu.VMEM((qa, nvir), f32)],
+        compiler_params=pltpu.CompilerParams(vmem_limit_bytes=60 * 2**20),
         name="pair_tiles",
-    )(metas[:, :1, :], occ_energy[ids], gt, cols, va, virt_energy[None, :])
+    )(metas, i_plan, occ_energy, gt, cols, virt_row)
 
     summed = lax.all_to_all(parts, "grp", split_axis=0, concat_axis=0, tiled=True)
     summed = summed.reshape(nvir, nvir)
-    fock = jnp.diag(virt_energy) + 0.5 * (fock_off + fock_off.T)
-    high = fock.astype(jnp.bfloat16)
-    low = (fock - high.astype(f32)).astype(jnp.bfloat16)
+    high, low = pl.pallas_call(
+        split_kernel,
+        out_shape=[jax.ShapeDtypeStruct((nvir, nvir), jnp.bfloat16)] * 2,
+        in_specs=[vmem] * 2,
+        out_specs=[vmem] * 2,
+        cost_estimate=pl.CostEstimate(flops=4 * nvir * nvir, bytes_accessed=8 * nvir * nvir, transcendentals=0),
+        name="fock_split",
+    )(virt_row, fock_off)
     residual = pl.pallas_call(
         fock_kernel,
         out_shape=jax.ShapeDtypeStruct((nvir, nvir), f32),

time: 107 us -> 106 us (level)
  Pallas kernels: 83.6 us -> 91.2 us
  local copies, waits for them, and re-layouts: 9.59 us -> 4.35 us
  other arithmetic: 4.21 us -> 0 us
    pallas_call x1 -> x2, Pallas kernels: 10.9 us -> 17.8 us  [the longest x1 15.3 us: shards(): pl.pallas_call(functools.partial(tiles_kernel, nt, group, no), grid=(nt /...]
    convert_element_type x2 -> x0, other arithmetic: 2.2 us -> none  [the longest x1 1.54 us: shards(): low = (fock - high.astype(f32)).astype(jnp.bfloat16)]
    another operation x1 -> x0, other arithmetic: 1.29 us -> none
    dynamic_slice x1 -> x0, local copies, waits for them, and re-layouts: 1.23 us -> none  [shards(): own_energy = lax.dynamic_slice_in_dim(occ_energy, me, 1)]
    unnamed x9 -> x4, local copies, waits for them, and re-layouts: 3.21 us -> 2.08 us
  transfers between devices with their start and end apart: 1 -> 1, of which waited for: 1 -> 1; matrix products, arithmetic and copies ran while one was open for 3% -> 0% of each run, Pallas kernels for 0% -> 2%
where the time goes in v2:
time: 106 us; the launch traced here: 105 us
  Pallas kernels  91.2 us (86%)
  waiting for transfers between devices  6.25 us (6%)
  local copies, waits for them, and re-layouts  4.35 us (4%)
  starting transfers between devices  3.47 us (3%)
    pallas_call x1, Pallas kernels, shards(): pl.pallas_call(functools.partial(gather_kernel, ng, no, nt), out_shape=[j...  71.2 us
    pallas_call x1, Pallas kernels, shards(): pl.pallas_call(functools.partial(tiles_kernel, nt, group, no), grid=(nt /...  15.3 us
    all_to_all x1, waiting for transfers between devices, shards(): lax.all_to_all(parts, 'grp', split_axis=0, concat_axis=0, tiled=True)  6.25 us
    all_to_all x1, starting transfers between devices, shards(): lax.all_to_all(parts, 'grp', split_axis=0, concat_axis=0, tiled=True)  3.47 us
    pallas_call x1, Pallas kernels, shards(): pl.pallas_call(split_kernel, out_shape=[jax.ShapeDtypeStruct((nvir, nvir)...  2.57 us
    transpose x1, local copies, waits for them, and re-layouts, shards(): gt, cols, metas = pl.pallas_call(functools.partial(gather_kernel, ng, no,...  2.26 us
    pallas_call x1, Pallas kernels, shards(): pl.pallas_call(fock_kernel, out_shape=jax.ShapeDtypeStruct((nvir, nvir),...  2.22 us
  transfers between devices with their start and end apart: 1, of which 1 were waited for; matrix products, arithmetic and copies ran while one was open for 0% of the time, Pallas kernels for 2%

profile of v2, /device:TPU:0, one launch (start us, length us, event | category | flops | bytes accessed | tf_op | source)
XLA Modules:
  0.0 105.3 jit_solution(3243513497949402658)
XLA Ops:
  0.0 2.3 %copy.8.panel_t = bf16[512,1024]{1,0:T(8,128)(2,1)} copy(bf16[512,1024]{0,1:T(8,128)(2,1)} %bitcast.9) | data formatting | bytes 2097152 | tf_op jit(solution)/shard_map/transpose | solution.py:299
  2.3 71.2 %gather_panels.1 = (bf16[12,128,1024]{2,1,0:T(8,128)(2,1)}, bf16[4,1024,512]{2,1,0:T(8,128)(2,1)}, f32[4,8,128]{2,1,0:T(8,128)}) custom-call(s32[3,4]{1,0:T(4,128)} %plan.3, f32[1,12]{1,0:T(1,128)} %bitcast.13, s32[1,12]{1,0:T(1,128)} %bitcast.14, bf16[512,1024]{1,0:T(8,128)(2,1)} %copy.8.panel_t, bf16[1024,512]{1,0:T(8,128)(2,1)} %bitcast.10), custom_call_target="tpu_custom_call" | custom-call | tf_op jit(solution)/shard_map/gather_panels/pallas_call | solution.py:273
  73.4 15.3 %pair_tiles.1 = bf16[4,128,512]{2,1,0:T(8,128)(2,1)} custom-call(f32[4,8,128]{2,1,0:T(8,128)} %get-tuple-element.10.metas, s32[3,4]{1,0:T(4,128)} %plan.3, f32[32]{0:T(128)} %occ.1, bf16[12,128,1024]{2,1,0:T(8,128)(2,1)} %get-tuple-element.11.gt, bf16[4,1024,512]{2,1,0:T(8,128)(2,1)} %get-tuple-element.12.cols, f32[1,512]{1,0:T(1,128)} %bitcast.11), custom_call_target="tpu_custom_call" | custom-call | tf_op jit(solution)/shard_map/pair_tiles/pallas_call | solution.py:303
  88.7 3.5 %all-to-all-start = ((bf16[4,128,512]{2,1,0:T(8,128)(2,1)}), bf16[4,128,512]{2,1,0:T(8,128)(2,1)S(1)}, u32[]{:S(2)}, u32[]{:S(2)}) async-start(bf16[4,128,512]{2,1,0:T(8,128)(2,1)} %pair_tiles.1), calls=%async_computation | async-start | bytes 1048576 | tf_op jit(solution)/shard_map/all_to_all | solution.py:321
  92.2 2.6 %fock_split.1 = (bf16[512,512]{1,0:T(8,128)(2,1)}, bf16[512,512]{1,0:T(8,128)(2,1)}) custom-call(f32[1,512]{1,0:T(1,128)} %bitcast.12, f32[512,512]{1,0:T(8,128)} %off.1), custom_call_target="tpu_custom_call" | custom-call | flops 1048576 | bytes 2097152 | tf_op jit(solution)/shard_map/fock_split/pallas_call | solution.py:323
  94.8 6.2 %all-to-all-done = bf16[4,128,512]{2,1,0:T(8,128)(2,1)S(1)} async-done(((bf16[4,128,512]{2,1,0:T(8,128)(2,1)}), bf16[4,128,512]{2,1,0:T(8,128)(2,1)S(1)}, u32[]{:S(2)}, u32[]{:S(2)}) %all-to-all-start) | async-done | bytes 524320 | tf_op jit(solution)/shard_map/all_to_all | solution.py:321
  101.0 0.0 copy-start
  101.0 1.0 copy-done
  102.0 0.0 copy-start.1
  102.1 1.0 copy-done.1
  103.1 2.2 %fock_products.1 = f32[512,512]{1,0:T(8,128)} custom-call(bf16[512,512]{1,0:T(8,128)(2,1)S(1)} %bitcast.8, bf16[512,512]{1,0:T(8,128)(2,1)S(1)} %copy-done, bf16[512,512]{1,0:T(8,128)(2,1)S(1)} %copy-done.1), custom_call_target="tpu_custom_call" | custom-call | tf_op jit(solution)/shard_map/fock_products/pallas_call | solution.py:331
Async XLA Ops:
  88.7 12.3 %all-to-all-start = ((bf16[4,128,512]{2,1,0:T(8,128)(2,1)}), bf16[4,128,512]{2,1,0:T(8,128)(2,1)S(1)}, u32[]{:S(2)}, u32[]{:S(2)}) async-start(bf16[4,128,512]{2,1,0:T(8,128)(2,1)} %pair_tiles.1), calls=%async_computation | async-start | bytes 1048576 | tf_op jit(solution)/shard_map/all_to_all | solution.py:321
  101.0 1.0 copy-start
  102.0 1.0 copy-start.1

commit v3 on v2

--- a/solution.py
+++ b/solution.py
@@ -167,7 +167,7 @@
                     if step > 0:
                         ring(way, step - 1, hf).wait_recv()
                     ring(way, step, hf).start()
-        if step == 0:
+        if step == steps // 2:
             across.wait_recv()
             onward = column(2, cols.at[x_peer], x_peer, core_peer)
             onward.start()
@@ -202,15 +202,14 @@
 
 
 def tiles_kernel(nt, group, no, metas, plan, occ, gt, cols, virt, out, acc, base):
-    part = pl.program_id(0)
-    j = pl.program_id(1)
+    j = pl.program_id(0)
     ng = out.shape[0]
     qa = gt.shape[1]
     steps = nt // ng
     g = lax.axis_index("grp")
     o = lax.axis_index("orb")
 
-    @pl.when((j == 0) & (part == 0))
+    @pl.when(j == 0)
     def _():
         acc[...] = jnp.zeros_like(acc)
         rows = jnp.broadcast_to(virt[:, pl.ds(pl.multiple_of(g * qa, 128), qa)], (qa, qa)).T
@@ -219,21 +218,22 @@
             base[:, at] = rows + virt[:, at]
 
     own = occ[j * no + o]
-    left = gt[...].reshape(group * qa, gt.shape[2])
-    integral = jnp.dot(left, cols[0], preferred_element_type=jnp.float32)
-    for k in range(group):
-        slot = part * group + k
-        hf, rest = slot // (nt // 2), lax.rem(slot, nt // 2)
-        c, s = rest // steps, lax.rem(rest, steps)
-        h = lax.rem(g // 2 + hf, 2) * 2 + c
-        t = s * ng + h
-        weight = metas[j, 0, t]
-        owner = metas[j, 1, t].astype(jnp.int32)
-        denominator = base[...] - occ[h * no + plan[s, h]] - own
-        amplitude = integral[k * qa : (k + 1) * qa] / denominator * weight
-        acc[owner] = acc[owner] + amplitude.astype(jnp.bfloat16).astype(jnp.float32)
-
-    @pl.when((j == ng - 1) & (part == pl.num_programs(0) - 1))
+    right = cols[0]
+    for first in range(0, nt, group):
+        left = gt[first : first + group].reshape(group * qa, gt.shape[2])
+        integral = jnp.dot(left, right, preferred_element_type=jnp.float32)
+        for k in range(group):
+            hf, rest = divmod(first + k, nt // 2)
+            c, s = divmod(rest, steps)
+            h = lax.rem(g // 2 + hf, 2) * 2 + c
+            t = s * ng + h
+            weight = metas[j, 0, t]
+            owner = metas[j, 1, t].astype(jnp.int32)
+            denominator = base[...] - occ[h * no + plan[s, h]] - own
+            amplitude = integral[k * qa : (k + 1) * qa] / denominator * weight
+            acc[owner] = acc[owner] + amplitude.astype(jnp.bfloat16).astype(jnp.float32)
+
+    @pl.when(j == ng - 1)
     def _():
         out[...] = acc[...].astype(out.dtype)
 
@@ -302,14 +302,14 @@
     group = 4
     parts = pl.pallas_call(
         functools.partial(tiles_kernel, nt, group, no),
-        grid=(nt // group, ng),
+        grid=(ng,),
         out_shape=jax.ShapeDtypeStruct((ng, qa, nvir), jnp.bfloat16),
         in_specs=[
             smem,
             smem,
             smem,
-            pl.BlockSpec((group, qa, naux), lambda p, j: (p, 0, 0)),
-            pl.BlockSpec((1, naux, nvir), lambda p, j: (j, 0, 0)),
+            vmem,
+            pl.BlockSpec((1, naux, nvir), lambda j: (j, 0, 0)),
             vmem,
         ],
         out_specs=vmem,
@@ -333,7 +333,7 @@
         out_shape=jax.ShapeDtypeStruct((nvir, nvir), f32),
         in_specs=[vmem] * 3,
         out_specs=vmem,
-        compiler_params=pltpu.CompilerParams(vmem_limit_bytes=48 * 2**20),
+        compiler_params=pltpu.CompilerParams(vmem_limit_bytes=60 * 2**20),
         name="fock_products",
     )(summed, high, low)
     return residual[None]

time: 106 us -> 97.5 us (0.920)
  Pallas kernels: 91.2 us -> 84.4 us
  local copies, waits for them, and re-layouts: 4.35 us -> 3.06 us
    pallas_call x1, Pallas kernels: 71.2 us -> 66.6 us  [shards(): pl.pallas_call(functools.partial(gather_kernel, ng, no, nt), out_shape=[j...]
    pallas_call x1, Pallas kernels: 15.3 us -> 11.7 us  [shards(): pl.pallas_call(functools.partial(tiles_kernel, nt, group, no), grid=(ng,)...]
    pallas_call x1, Pallas kernels: 2.22 us -> 3.57 us  [shards(): pl.pallas_call(fock_kernel, out_shape=jax.ShapeDtypeStruct((nvir, nvir),...]
    unnamed x4 -> x2, local copies, waits for them, and re-layouts: 2.08 us -> 0.8 us
  transfers between devices with their start and end apart: 1 -> 1, of which waited for: 1 -> 1; matrix products, arithmetic and copies ran while one was open for 0% -> 0% of each run, Pallas kernels for 2% -> 3%
where the time goes in v3:
time: 97.5 us; the launch traced here: 97.2 us
  Pallas kernels  84.4 us (87%)
  waiting for transfers between devices  6.24 us (6%)
  starting transfers between devices  3.47 us (4%)
  local copies, waits for them, and re-layouts  3.06 us (3%)
    pallas_call x1, Pallas kernels, shards(): pl.pallas_call(functools.partial(gather_kernel, ng, no, nt), out_shape=[j...  66.6 us
    pallas_call x1, Pallas kernels, shards(): pl.pallas_call(functools.partial(tiles_kernel, nt, group, no), grid=(ng,)...  11.7 us
    all_to_all x1, waiting for transfers between devices, shards(): lax.all_to_all(parts, 'grp', split_axis=0, concat_axis=0, tiled=True)  6.24 us
    pallas_call x1, Pallas kernels, shards(): pl.pallas_call(fock_kernel, out_shape=jax.ShapeDtypeStruct((nvir, nvir),...  3.57 us
    all_to_all x1, starting transfers between devices, shards(): lax.all_to_all(parts, 'grp', split_axis=0, concat_axis=0, tiled=True)  3.47 us
    pallas_call x1, Pallas kernels, shards(): pl.pallas_call(split_kernel, out_shape=[jax.ShapeDtypeStruct((nvir, nvir)...  2.57 us
    transpose x1, local copies, waits for them, and re-layouts, shards(): gt, cols, metas = pl.pallas_call(functools.partial(gather_kernel, ng, no,...  2.26 us
  transfers between devices with their start and end apart: 1, of which 1 were waited for; matrix products, arithmetic and copies ran while one was open for 0% of the time, Pallas kernels for 3%

profile of v3, /device:TPU:0, one launch (start us, length us, event | category | flops | bytes accessed | tf_op | source)
XLA Modules:
  0.0 97.2 jit_solution(14064559338127686088)
XLA Ops:
  0.0 2.3 %copy.8.panel_t = bf16[512,1024]{1,0:T(8,128)(2,1)} copy(bf16[512,1024]{0,1:T(8,128)(2,1)} %bitcast.8) | data formatting | bytes 2097152 | tf_op jit(solution)/shard_map/transpose | solution.py:299
  2.3 66.6 %gather_panels.1 = (bf16[12,128,1024]{2,1,0:T(8,128)(2,1)}, bf16[4,1024,512]{2,1,0:T(8,128)(2,1)}, f32[4,8,128]{2,1,0:T(8,128)}) custom-call(s32[3,4]{1,0:T(4,128)} %plan.3, f32[1,12]{1,0:T(1,128)} %bitcast.13, s32[1,12]{1,0:T(1,128)} %bitcast.14, bf16[512,1024]{1,0:T(8,128)(2,1)} %copy.8.panel_t, bf16[1024,512]{1,0:T(8,128)(2,1)} %bitcast.9), custom_call_target="tpu_custom_call" | custom-call | tf_op jit(solution)/shard_map/gather_panels/pallas_call | solution.py:273
  68.8 11.7 %pair_tiles.1 = bf16[4,128,512]{2,1,0:T(8,128)(2,1)} custom-call(f32[4,8,128]{2,1,0:T(8,128)} %get-tuple-element.10.metas, s32[3,4]{1,0:T(4,128)} %plan.3, f32[32]{0:T(128)} %occ.1, bf16[12,128,1024]{2,1,0:T(8,128)(2,1)} %get-tuple-element.11.gt, bf16[4,1024,512]{2,1,0:T(8,128)(2,1)} %get-tuple-element.12.cols, f32[1,512]{1,0:T(1,128)} %bitcast.11), custom_call_target="tpu_custom_call" | custom-call | tf_op jit(solution)/shard_map/pair_tiles/pallas_call | solution.py:303
  80.5 3.5 %all-to-all-start = ((bf16[4,128,512]{2,1,0:T(8,128)(2,1)}), bf16[4,128,512]{2,1,0:T(8,128)(2,1)S(1)}, u32[]{:S(2)}, u32[]{:S(2)}) async-start(bf16[4,128,512]{2,1,0:T(8,128)(2,1)} %pair_tiles.1), calls=%async_computation | async-start | bytes 1048576 | tf_op jit(solution)/shard_map/all_to_all | solution.py:321
  84.0 2.6 %fock_split.1 = (bf16[512,512]{1,0:T(8,128)(2,1)}, bf16[512,512]{1,0:T(8,128)(2,1)}) custom-call(f32[1,512]{1,0:T(1,128)} %bitcast.12, f32[512,512]{1,0:T(8,128)} %off.1), custom_call_target="tpu_custom_call" | custom-call | flops 1048576 | bytes 2097152 | tf_op jit(solution)/shard_map/fock_split/pallas_call | solution.py:323
  86.6 6.2 %all-to-all-done = bf16[4,128,512]{2,1,0:T(8,128)(2,1)S(1)} async-done(((bf16[4,128,512]{2,1,0:T(8,128)(2,1)}), bf16[4,128,512]{2,1,0:T(8,128)(2,1)S(1)}, u32[]{:S(2)}, u32[]{:S(2)}) %all-to-all-start) | async-done | bytes 524320 | tf_op jit(solution)/shard_map/all_to_all | solution.py:321
  92.8 0.0 copy-start
  92.8 0.8 copy-done
  93.6 3.6 %fock_products.1 = f32[512,512]{1,0:T(8,128)} custom-call(bf16[512,512]{1,0:T(8,128)(2,1)} %bitcast.10, bf16[512,512]{1,0:T(8,128)(2,1)} %get-tuple-element.13.high, bf16[512,512]{1,0:T(8,128)(2,1)} %get-tuple-element.14.low), custom_call_target="tpu_custom_call" | custom-call | tf_op jit(solution)/shard_map/fock_products/pallas_call | solution.py:331
Async XLA Ops:
  80.5 12.3 %all-to-all-start = ((bf16[4,128,512]{2,1,0:T(8,128)(2,1)}), bf16[4,128,512]{2,1,0:T(8,128)(2,1)S(1)}, u32[]{:S(2)}, u32[]{:S(2)}) async-start(bf16[4,128,512]{2,1,0:T(8,128)(2,1)} %pair_tiles.1), calls=%async_computation | async-start | bytes 1048576 | tf_op jit(solution)/shard_map/all_to_all | solution.py:321
  92.8 0.8 copy-start

commit v4 on v3

--- a/solution.py
+++ b/solution.py
@@ -167,7 +167,7 @@
                     if step > 0:
                         ring(way, step - 1, hf).wait_recv()
                     ring(way, step, hf).start()
-        if step == steps // 2:
+        if step == steps - 1:
             across.wait_recv()
             onward = column(2, cols.at[x_peer], x_peer, core_peer)
             onward.start()

time: 97.5 us -> 97.5 us (level)
  no operation moved by 1% of the time
where the time goes in v4:
time: 97.5 us; the launch traced here: 97.2 us
  Pallas kernels  84.4 us (87%)
  waiting for transfers between devices  6.24 us (6%)
  starting transfers between devices  3.47 us (4%)
  local copies, waits for them, and re-layouts  3.06 us (3%)
    pallas_call x1, Pallas kernels, shards(): pl.pallas_call(functools.partial(gather_kernel, ng, no, nt), out_shape=[j...  66.6 us
    pallas_call x1, Pallas kernels, shards(): pl.pallas_call(functools.partial(tiles_kernel, nt, group, no), grid=(ng,)...  11.7 us
    all_to_all x1, waiting for transfers between devices, shards(): lax.all_to_all(parts, 'grp', split_axis=0, concat_axis=0, tiled=True)  6.24 us
    pallas_call x1, Pallas kernels, shards(): pl.pallas_call(fock_kernel, out_shape=jax.ShapeDtypeStruct((nvir, nvir),...  3.57 us
    all_to_all x1, starting transfers between devices, shards(): lax.all_to_all(parts, 'grp', split_axis=0, concat_axis=0, tiled=True)  3.47 us
    pallas_call x1, Pallas kernels, shards(): pl.pallas_call(split_kernel, out_shape=[jax.ShapeDtypeStruct((nvir, nvir)...  2.57 us
    transpose x1, local copies, waits for them, and re-layouts, shards(): gt, cols, metas = pl.pallas_call(functools.partial(gather_kernel, ng, no,...  2.26 us
  transfers between devices with their start and end apart: 1, of which 1 were waited for; matrix products, arithmetic and copies ran while one was open for 0% of the time, Pallas kernels for 3%

profile of v4, /device:TPU:0, one launch (start us, length us, event | category | flops | bytes accessed | tf_op | source)
XLA Modules:
  0.0 97.2 jit_solution(11568599349780313944)
XLA Ops:
  0.0 2.3 %copy.8.panel_t = bf16[512,1024]{1,0:T(8,128)(2,1)} copy(bf16[512,1024]{0,1:T(8,128)(2,1)} %bitcast.8) | data formatting | bytes 2097152 | tf_op jit(solution)/shard_map/transpose | solution.py:299
  2.3 66.6 %gather_panels.1 = (bf16[12,128,1024]{2,1,0:T(8,128)(2,1)}, bf16[4,1024,512]{2,1,0:T(8,128)(2,1)}, f32[4,8,128]{2,1,0:T(8,128)}) custom-call(s32[3,4]{1,0:T(4,128)} %plan.3, f32[1,12]{1,0:T(1,128)} %bitcast.13, s32[1,12]{1,0:T(1,128)} %bitcast.14, bf16[512,1024]{1,0:T(8,128)(2,1)} %copy.8.panel_t, bf16[1024,512]{1,0:T(8,128)(2,1)} %bitcast.9), custom_call_target="tpu_custom_call" | custom-call | tf_op jit(solution)/shard_map/gather_panels/pallas_call | solution.py:273
  68.8 11.7 %pair_tiles.1 = bf16[4,128,512]{2,1,0:T(8,128)(2,1)} custom-call(f32[4,8,128]{2,1,0:T(8,128)} %get-tuple-element.10.metas, s32[3,4]{1,0:T(4,128)} %plan.3, f32[32]{0:T(128)} %occ.1, bf16[12,128,1024]{2,1,0:T(8,128)(2,1)} %get-tuple-element.11.gt, bf16[4,1024,512]{2,1,0:T(8,128)(2,1)} %get-tuple-element.12.cols, f32[1,512]{1,0:T(1,128)} %bitcast.11), custom_call_target="tpu_custom_call" | custom-call | tf_op jit(solution)/shard_map/pair_tiles/pallas_call | solution.py:303
  80.5 3.5 %all-to-all-start = ((bf16[4,128,512]{2,1,0:T(8,128)(2,1)}), bf16[4,128,512]{2,1,0:T(8,128)(2,1)S(1)}, u32[]{:S(2)}, u32[]{:S(2)}) async-start(bf16[4,128,512]{2,1,0:T(8,128)(2,1)} %pair_tiles.1), calls=%async_computation | async-start | bytes 1048576 | tf_op jit(solution)/shard_map/all_to_all | solution.py:321
  84.0 2.6 %fock_split.1 = (bf16[512,512]{1,0:T(8,128)(2,1)}, bf16[512,512]{1,0:T(8,128)(2,1)}) custom-call(f32[1,512]{1,0:T(1,128)} %bitcast.12, f32[512,512]{1,0:T(8,128)} %off.1), custom_call_target="tpu_custom_call" | custom-call | flops 1048576 | bytes 2097152 | tf_op jit(solution)/shard_map/fock_split/pallas_call | solution.py:323
  86.6 6.2 %all-to-all-done = bf16[4,128,512]{2,1,0:T(8,128)(2,1)S(1)} async-done(((bf16[4,128,512]{2,1,0:T(8,128)(2,1)}), bf16[4,128,512]{2,1,0:T(8,128)(2,1)S(1)}, u32[]{:S(2)}, u32[]{:S(2)}) %all-to-all-start) | async-done | bytes 524320 | tf_op jit(solution)/shard_map/all_to_all | solution.py:321
  92.8 0.0 copy-start
  92.8 0.8 copy-done
  93.6 3.6 %fock_products.1 = f32[512,512]{1,0:T(8,128)} custom-call(bf16[512,512]{1,0:T(8,128)(2,1)} %bitcast.10, bf16[512,512]{1,0:T(8,128)(2,1)} %get-tuple-element.13.high, bf16[512,512]{1,0:T(8,128)(2,1)} %get-tuple-element.14.low), custom_call_target="tpu_custom_call" | custom-call | tf_op jit(solution)/shard_map/fock_products/pallas_call | solution.py:331
Async XLA Ops:
  80.5 12.3 %all-to-all-start = ((bf16[4,128,512]{2,1,0:T(8,128)(2,1)}), bf16[4,128,512]{2,1,0:T(8,128)(2,1)S(1)}, u32[]{:S(2)}, u32[]{:S(2)}) async-start(bf16[4,128,512]{2,1,0:T(8,128)(2,1)} %pair_tiles.1), calls=%async_computation | async-start | bytes 1048576 | tf_op jit(solution)/shard_map/all_to_all | solution.py:321
  92.8 0.8 copy-start

commit v5 on v3

--- a/solution.py
+++ b/solution.py
@@ -238,7 +238,24 @@
         out[...] = acc[...].astype(out.dtype)
 
 
-def split_kernel(virt, off, high, low):
+def exchange_kernel(ng, parts, virt, off, summed, high, low, send, recv, loc):
+    g = lax.axis_index("grp")
+    o = lax.axis_index("orb")
+    copies = []
+    for k in range(ng - 1, 0, -1):
+        to = lax.rem(g + k, ng)
+        copy = pltpu.make_async_remote_copy(
+            src_ref=parts.at[to],
+            dst_ref=summed.at[g],
+            send_sem=send.at[k],
+            recv_sem=recv.at[k],
+            device_id=(to, o),
+            device_id_type=MESH,
+        )
+        copy.start()
+        copies.append(copy)
+    own = pltpu.make_async_copy(parts.at[g], summed.at[g], loc.at[0])
+    own.start()
     n = off.shape[0]
     rows = lax.broadcasted_iota(jnp.int32, (n, n), 0)
     columns = lax.broadcasted_iota(jnp.int32, (n, n), 1)
@@ -246,6 +263,9 @@
     top = fock.astype(jnp.bfloat16)
     high[...] = top
     low[...] = (fock - top.astype(jnp.float32)).astype(jnp.bfloat16)
+    own.wait()
+    for copy in copies:
+        copy.wait()
 
 
 def fock_kernel(summed, high, low, out):
@@ -318,16 +338,17 @@
         name="pair_tiles",
     )(metas, i_plan, occ_energy, gt, cols, virt_row)
 
-    summed = lax.all_to_all(parts, "grp", split_axis=0, concat_axis=0, tiled=True)
+    summed, high, low = pl.pallas_call(
+        functools.partial(exchange_kernel, ng),
+        out_shape=[jax.ShapeDtypeStruct((ng, qa, nvir), jnp.bfloat16)]
+        + [jax.ShapeDtypeStruct((nvir, nvir), jnp.bfloat16)] * 2,
+        in_specs=[hbm, vmem, vmem],
+        out_specs=[hbm, vmem, vmem],
+        scratch_shapes=[dma((ng,)), dma((ng,)), dma((1,))],
+        compiler_params=pltpu.CompilerParams(has_side_effects=True),
+        name="exchange_sums",
+    )(parts, virt_row, fock_off)
     summed = summed.reshape(nvir, nvir)
-    high, low = pl.pallas_call(
-        split_kernel,
-        out_shape=[jax.ShapeDtypeStruct((nvir, nvir), jnp.bfloat16)] * 2,
-        in_specs=[vmem] * 2,
-        out_specs=[vmem] * 2,
-        cost_estimate=pl.CostEstimate(flops=4 * nvir * nvir, bytes_accessed=8 * nvir * nvir, transcendentals=0),
-        name="fock_split",
-    )(virt_row, fock_off)
     residual = pl.pallas_call(
         fock_kernel,
         out_shape=jax.ShapeDtypeStruct((nvir, nvir), f32),

time: 97.5 us -> 98.8 us (1.013)
  Pallas kernels: 84.4 us -> 96.2 us
  waiting for transfers between devices: 6.24 us -> 0 us
  starting transfers between devices: 3.47 us -> 0 us
    pallas_call x1, Pallas kernels: 2.57 us -> 14.4 us  [shards(): pl.pallas_call(functools.partial(exchange_kernel, ng), out_shape=[jax.Sha...]
    all_to_all x1 -> x0, waiting for transfers between devices: 6.24 us -> none  [shards(): lax.all_to_all(parts, 'grp', split_axis=0, concat_axis=0, tiled=True)]
    all_to_all x1 -> x0, starting transfers between devices: 3.47 us -> none  [shards(): lax.all_to_all(parts, 'grp', split_axis=0, concat_axis=0, tiled=True)]
  transfers between devices with their start and end apart: 1 -> 0, of which waited for: 1 -> 0; matrix products, arithmetic and copies ran while one was open for 0% -> 0% of each run, Pallas kernels for 3% -> 0%
where the time goes in v5:
time: 98.8 us; the launch traced here: 98.5 us
  Pallas kernels  96.2 us (97%)
  local copies, waits for them, and re-layouts  2.26 us (2%)
    pallas_call x1, Pallas kernels, shards(): pl.pallas_call(functools.partial(gather_kernel, ng, no, nt), out_shape=[j...  66.6 us
    pallas_call x1, Pallas kernels, shards(): pl.pallas_call(functools.partial(exchange_kernel, ng), out_shape=[jax.Sha...  14.4 us
    pallas_call x1, Pallas kernels, shards(): pl.pallas_call(functools.partial(tiles_kernel, nt, group, no), grid=(ng,)...  11.7 us
    pallas_call x1, Pallas kernels, shards(): pl.pallas_call(fock_kernel, out_shape=jax.ShapeDtypeStruct((nvir, nvir),...  3.58 us
    transpose x1, local copies, waits for them, and re-layouts, shards(): gt, cols, metas = pl.pallas_call(functools.partial(gather_kernel, ng, no,...  2.26 us

profile of v5, /device:TPU:0, one launch (start us, length us, event | category | flops | bytes accessed | tf_op | source)
XLA Modules:
  0.0 98.5 jit_solution(5335093160586839635)
XLA Ops:
  0.0 2.3 %copy.8.panel_t = bf16[512,1024]{1,0:T(8,128)(2,1)} copy(bf16[512,1024]{0,1:T(8,128)(2,1)} %bitcast.8) | data formatting | bytes 2097152 | tf_op jit(solution)/shard_map/transpose | solution.py:319
  2.3 66.6 %gather_panels.1 = (bf16[12,128,1024]{2,1,0:T(8,128)(2,1)}, bf16[4,1024,512]{2,1,0:T(8,128)(2,1)}, f32[4,8,128]{2,1,0:T(8,128)}) custom-call(s32[3,4]{1,0:T(4,128)} %plan.3, f32[1,12]{1,0:T(1,128)} %bitcast.13, s32[1,12]{1,0:T(1,128)} %bitcast.14, bf16[512,1024]{1,0:T(8,128)(2,1)} %copy.8.panel_t, bf16[1024,512]{1,0:T(8,128)(2,1)} %bitcast.9), custom_call_target="tpu_custom_call" | custom-call | tf_op jit(solution)/shard_map/gather_panels/pallas_call | solution.py:293
  68.8 11.7 %pair_tiles.1.parts = bf16[4,128,512]{2,1,0:T(8,128)(2,1)} custom-call(f32[4,8,128]{2,1,0:T(8,128)} %get-tuple-element.11.metas, s32[3,4]{1,0:T(4,128)} %plan.3, f32[32]{0:T(128)} %occ.1, bf16[12,128,1024]{2,1,0:T(8,128)(2,1)} %get-tuple-element.12.gt, bf16[4,1024,512]{2,1,0:T(8,128)(2,1)} %get-tuple-element.13.cols, f32[1,512]{1,0:T(1,128)} %bitcast.11), custom_call_target="tpu_custom_call" | custom-call | tf_op jit(solution)/shard_map/pair_tiles/pallas_call | solution.py:323
  80.5 14.4 %exchange_sums.1 = (bf16[4,128,512]{2,1,0:T(8,128)(2,1)}, bf16[512,512]{1,0:T(8,128)(2,1)}, bf16[512,512]{1,0:T(8,128)(2,1)}) custom-call(bf16[4,128,512]{2,1,0:T(8,128)(2,1)} %pair_tiles.1.parts, f32[1,512]{1,0:T(1,128)} %bitcast.12, f32[512,512]{1,0:T(8,128)} %off.1), custom_call_target="tpu_custom_call" | custom-call | tf_op jit(solution)/shard_map/exchange_sums/pallas_call | solution.py:341
  94.9 3.6 %fock_products.1 = f32[512,512]{1,0:T(8,128)} custom-call(bf16[512,512]{1,0:T(8,128)(2,1)} %bitcast.10, bf16[512,512]{1,0:T(8,128)(2,1)} %get-tuple-element.15.high, bf16[512,512]{1,0:T(8,128)(2,1)} %get-tuple-element.16.low), custom_call_target="tpu_custom_call" | custom-call | tf_op jit(solution)/shard_map/fock_products/pallas_call | solution.py:352
